TPU v7x, 256 devices: a whole 4x4x8 slice. The times are simulated.
256 devices in a mesh: dp: 64 (over z, x, core), tensor: 4 (over y).
Axes of the slice: x: 4, y: 4, z: 8, core: 2. Of those that a mesh axis runs over, the one named last changes fastest.
Arguments:
- queries: bfloat16 [8192, 5120], P('dp', 'tensor'), may hold values from -200 to 200
- keys: bfloat16 [8192, 1024], P('dp', 'tensor'), may hold values from -8 to 8
- values: bfloat16 [8192, 1024], P('dp', 'tensor'), may hold values from -6 to 6
- output_gradient: bfloat16 [8192, 5120], P('dp', 'tensor'), may hold values from -6 to 6
- prompt_slot_keys: bfloat16 [2048, 1024], P('dp', 'tensor'), may hold values from -6 to 6
- prompt_slot_values: bfloat16 [2048, 1024], P('dp', 'tensor'), may hold values from -6 to 6
- query_weight: bfloat16 [5120, 5120], P('dp', 'tensor'), may hold values from -0.078125 to 0.078125
- lengths: int32 [128], replicated, may hold values from 1 to 128, 8192 in all
- prompt_owner: int32 [8], replicated, may hold values from 0 to 7, each once
Outputs:
- grad_queries: bfloat16 [8192, 5120], P('dp', 'tensor')
- grad_keys: bfloat16 [8192, 1024], P('dp', 'tensor')
- grad_values: bfloat16 [8192, 1024], P('dp', 'tensor')
- grad_prompt_keys: bfloat16 [2048, 1024], P('dp', 'tensor')
- grad_prompt_values: bfloat16 [2048, 1024], P('dp', 'tensor')
- grad_input: bfloat16 [8192, 5120], P('dp', 'tensor')
Inputs may be any that keep to these rules, and one draw needn't show every extreme that they name: `lengths`: lengths of the 128 responses in packing order; response r answers prompt r // 16; they sum to 8192 and the largest is exactly 128. A permutation: prompt p sits in slot prompt_owner[p], the rows p' * 256 to (p' + 1) * 256 - 1 of the prompt arrays with p' = prompt_owner[p].
All inputs are finite; a program needn't handle non-finite values.
Results may differ from a plain program's by a relative error of at most 0.015.
Values may be sent and summed in bfloat16 or wider, within the bound.
A program may use at most 64 MiB of HBM per device.

v0:
```python
import math

import jax
import jax.numpy as jnp
from jax import lax
from jax.sharding import PartitionSpec as P

QUERY_HEADS = 40
KEY_VALUE_HEADS = 8
HEAD_SIZE = 128
IMAGE_PROMPTS = 8
RESP_PER = 16


NEG = -1e30


def from_behind(value, axis, steps):
    count = lax.axis_size(axis)
    first, last = (max(0, -steps), min(count, count - steps))
    return lax.ppermute(value, axis, [(source, source + steps) for source in range(first, last)])


def row_labels(lengths, first_row, count):
    rows = first_row + jnp.arange(count, dtype=jnp.int32)
    ends = jnp.cumsum(lengths)
    before = ends[None, :] <= rows[:, None]
    resp = jnp.sum(before.astype(jnp.int32), axis=1)
    starts = jnp.sum(jnp.where(before, lengths[None, :], 0), axis=1)
    return (rows, starts, resp // RESP_PER)


def key_prompts(owner, first_key, count, plen):
    slots = (first_key + jnp.arange(count, dtype=jnp.int32)) // plen
    match = owner[None, :] == slots[:, None]
    return jnp.sum(jnp.where(match, jnp.arange(IMAGE_PROMPTS, dtype=jnp.int32)[None, :], 0), axis=1)


def forward_block(state, query_rows, kblock, vblock, mask):
    high, total, accum = state
    scale = 1.0 / math.sqrt(query_rows.shape[-1])
    scores = (
        jnp.einsum("rhgd,khd->hgrk", query_rows, kblock, preferred_element_type=jnp.float32) * scale
    )
    masked = jnp.where(mask[None, None], scores, NEG)
    newhigh = jnp.maximum(high, jnp.max(masked, axis=-1))
    weights = jnp.where(mask[None, None], jnp.exp(masked - newhigh[..., None]), 0.0)
    scale_factor = jnp.exp(high - newhigh)
    total = total * scale_factor + jnp.sum(weights, axis=-1)
    update = jnp.einsum(
        "hgrk,khd->rhgd", weights, vblock.astype(jnp.float32), precision=lax.Precision.HIGHEST
    )
    accum = accum * jnp.transpose(scale_factor, (2, 0, 1))[..., None] + update
    return (newhigh, total, accum)


def backward_block(query_rows, gradient_total, kblock, vblock, mask, lse, delta):
    scale = 1.0 / math.sqrt(query_rows.shape[-1])
    scores = (
        jnp.einsum("rhgd,khd->hgrk", query_rows, kblock, preferred_element_type=jnp.float32) * scale
    )
    prob = jnp.where(mask[None, None], jnp.exp(scores - lse[..., None]), 0.0)
    dprob = jnp.einsum("rhgd,khd->hgrk", gradient_total, vblock, preferred_element_type=jnp.float32)
    dscore = (prob * (dprob - delta[..., None])).astype(jnp.bfloat16)
    probw = prob.astype(jnp.bfloat16)
    dquery = (
        jnp.einsum("hgrk,khd->rhgd", dscore, kblock, preferred_element_type=jnp.float32) * scale
    )
    key_gradient = (
        jnp.einsum("hgrk,rhgd->khd", dscore, query_rows, preferred_element_type=jnp.float32) * scale
    )
    value_gradient = jnp.einsum(
        "hgrk,rhgd->khd", probw, gradient_total, preferred_element_type=jnp.float32
    )
    return (dquery, key_gradient, value_gradient)


def shards(
    queries,
    keys,
    values,
    output_gradient,
    prompt_slot_keys,
    prompt_slot_values,
    query_weight,
    lengths,
    prompt_owner,
):
    count = queries.shape[0]
    heads_kv = keys.shape[1] // HEAD_SIZE
    query_group = QUERY_HEADS // KEY_VALUE_HEADS
    query_rows = queries.reshape(count, heads_kv, query_group, HEAD_SIZE)
    gradient_total = output_gradient.reshape(count, heads_kv, query_group, HEAD_SIZE)
    first_row = lax.axis_index("dp") * count
    rows, starts, rprompt = row_labels(lengths, first_row, count)
    plen = prompt_slot_keys.shape[0] * lax.axis_size("dp") // IMAGE_PROMPTS
    prompt_rows = prompt_slot_keys.shape[0] * lax.axis_size("dp")

    def block_size(size):
        return math.gcd(size, 256)

    earlier = from_behind((keys, values), "dp", 1)
    wkeys = jnp.concatenate([earlier[0], keys], axis=0).reshape(2 * count, heads_kv, HEAD_SIZE)
    wvals = jnp.concatenate([earlier[1], values], axis=0).reshape(2 * count, heads_kv, HEAD_SIZE)
    wpos = first_row - count + jnp.arange(2 * count, dtype=jnp.int32)
    smask = (wpos[None, :] >= starts[:, None]) & (wpos[None, :] <= rows[:, None])
    initial_state = (
        jnp.full((heads_kv, query_group, count), NEG, jnp.float32),
        jnp.zeros((heads_kv, query_group, count), jnp.float32),
        jnp.zeros((count, heads_kv, query_group, HEAD_SIZE), jnp.float32),
    )
    state = forward_block(initial_state, query_rows, wkeys, wvals, smask)
    prompt_key_rows = lax.all_gather(prompt_slot_keys, "dp", axis=0, tiled=True)
    prompt_value_rows = lax.all_gather(prompt_slot_values, "dp", axis=0, tiled=True)
    size = prompt_key_rows.shape[0]
    width = block_size(size)

    def step(index, carry):
        offset = (index * width).astype(jnp.int32)
        kblock = lax.dynamic_slice_in_dim(prompt_key_rows, offset, width, 0).reshape(
            width, heads_kv, HEAD_SIZE
        )
        vblock = lax.dynamic_slice_in_dim(prompt_value_rows, offset, width, 0).reshape(
            width, heads_kv, HEAD_SIZE
        )
        kprompt = key_prompts(prompt_owner, offset, width, plen)
        mask = rprompt[:, None] == kprompt[None, :]
        return lax.cond(
            jnp.any(mask),
            lambda c: forward_block(c, query_rows, kblock, vblock, mask),
            lambda c: c,
            carry,
        )

    state = lax.fori_loop(0, size // width, step, state)
    high, total, accum = state
    lse = high + jnp.log(total)
    out = accum / jnp.transpose(total, (2, 0, 1))[..., None]
    delta = jnp.transpose(jnp.sum(gradient_total.astype(jnp.float32) * out, axis=-1), (1, 2, 0))
    dquery, dkey_w, dval_w = backward_block(
        query_rows, gradient_total, wkeys, wvals, smask, lse, delta
    )
    binit = (
        dquery,
        jnp.zeros((prompt_rows, heads_kv * HEAD_SIZE), jnp.float32),
        jnp.zeros((prompt_rows, heads_kv * HEAD_SIZE), jnp.float32),
    )
    prompt_prompt_key_rows = lax.all_gather(prompt_slot_keys, "dp", axis=0, tiled=True)
    prompt_prompt_value_rows = lax.all_gather(prompt_slot_values, "dp", axis=0, tiled=True)
    size = prompt_prompt_key_rows.shape[0]
    prompt_width = block_size(size)

    def step(index, inner):
        offset = (index * prompt_width).astype(jnp.int32)
        kblock = lax.dynamic_slice_in_dim(prompt_prompt_key_rows, offset, prompt_width, 0).reshape(
            prompt_width, heads_kv, HEAD_SIZE
        )
        vblock = lax.dynamic_slice_in_dim(
            prompt_prompt_value_rows, offset, prompt_width, 0
        ).reshape(prompt_width, heads_kv, HEAD_SIZE)
        kprompt = key_prompts(prompt_owner, offset, prompt_width, plen)
        mask = rprompt[:, None] == kprompt[None, :]

        def work(c):
            dq_now, gk_now, gv_now = c
            dq_part, dk_part, dv_part = backward_block(
                query_rows, gradient_total, kblock, vblock, mask, lse, delta
            )
            zero = jnp.zeros((), jnp.int32)
            cur_k = lax.dynamic_slice_in_dim(gk_now, offset, prompt_width, 0)
            cur_v = lax.dynamic_slice_in_dim(gv_now, offset, prompt_width, 0)
            gk_now = lax.dynamic_update_slice(
                gk_now, cur_k + dk_part.reshape(prompt_width, -1), (offset, zero)
            )
            gv_now = lax.dynamic_update_slice(
                gv_now, cur_v + dv_part.reshape(prompt_width, -1), (offset, zero)
            )
            return (dq_now + dq_part, gk_now, gv_now)

        return lax.cond(jnp.any(mask), work, lambda c: c, inner)

    dquery, gpk, gpv = lax.fori_loop(0, size // prompt_width, step, binit)
    dkey_w = dkey_w.reshape(2 * count, heads_kv * HEAD_SIZE)
    dval_w = dval_w.reshape(2 * count, heads_kv * HEAD_SIZE)
    arrived = (
        from_behind(dkey_w[:count].astype(jnp.bfloat16), "dp", -1).astype(jnp.float32),
        from_behind(dval_w[:count].astype(jnp.bfloat16), "dp", -1).astype(jnp.float32),
    )
    grad_keys = (dkey_w[count:] + arrived[0]).astype(jnp.bfloat16)
    grad_values = (dval_w[count:] + arrived[1]).astype(jnp.bfloat16)
    summed = (
        lax.psum_scatter(gpk, "dp", scatter_dimension=0, tiled=True),
        lax.psum_scatter(gpv, "dp", scatter_dimension=0, tiled=True),
    )
    grad_queries = dquery.reshape(count, heads_kv * query_group * HEAD_SIZE).astype(jnp.bfloat16)
    partial_input = lax.dot_general(
        grad_queries,
        lax.all_gather(query_weight, "dp", axis=0, tiled=True),
        (((1,), (1,)), ((), ())),
        preferred_element_type=jnp.float32,
    )
    grad_input = lax.psum_scatter(
        partial_input.astype(jnp.bfloat16), "tensor", scatter_dimension=1, tiled=True
    )
    return (
        grad_queries,
        grad_keys,
        grad_values,
        summed[0].astype(jnp.bfloat16),
        summed[1].astype(jnp.bfloat16),
        grad_input,
    )


def solution(mesh):
    placed = (
        P("dp", "tensor"),
        P("dp", "tensor"),
        P("dp", "tensor"),
        P("dp", "tensor"),
        P("dp", "tensor"),
        P("dp", "tensor"),
        P("dp", "tensor"),
        P(),
        P(),
    )
    return jax.shard_map(
        shards,
        mesh=mesh,
        in_specs=placed,
        out_specs=(
            P("dp", "tensor"),
            P("dp", "tensor"),
            P("dp", "tensor"),
            P("dp", "tensor"),
            P("dp", "tensor"),
            P("dp", "tensor"),
        ),
        check_vma=False,
    )
```

profile of v0, /device:TPU:1, one launch (start us, length us, event | category | flops | bytes accessed | tf_op | source)
XLA Modules:
  0.0 578.7 jit_solution(8371934710686567557)
XLA Ops:
  7.2 0.7 all-gather.4.cloned.1.call-update
  8.0 0.7 all-gather.6.cloned.1.call-update
  8.7 0.7 all-gather.8.cloned.1.call-update
  9.5 0.9 copy.135
  10.4 4.5 collective-permute-start
  14.9 1.9 collective-permute-start.1
  16.9 0.8 copy.137
  17.9 0.8 fusion.42
  18.9 1.2 copy.147
  21.4 1.8 fusion.28
  23.2 1.3 copy.143
  24.5 66.8 %all-gather.4.cloned.1.call-done = bf16[2048,256]{1,0:T(8,128)(2,1)} async-done(((bf16[32,256]{1,0:T(8,128)(2,1)}), bf16[2048,256]{1,0:T(8,128)(2,1)}) %all-gather.4.cloned.1.call-update) | async-done | bytes 1048592 | tf_op jit(solution)/shard_map/all_gather | solution.py:113
  91.4 2.3 copy.144
  93.6 74.6 %all-gather.6.cloned.1.call-done = bf16[2048,256]{1,0:T(8,128)(2,1)} async-done(((bf16[32,256]{1,0:T(8,128)(2,1)}), bf16[2048,256]{1,0:T(8,128)(2,1)}) %all-gather.6.cloned.1.call-update) | async-done | bytes 1048592 | tf_op jit(solution)/shard_map/all_gather | solution.py:114
  168.2 2.3 copy.146
  170.5 15.3 %while.38 = (s32[]{:T(128)}, f32[2,5,128]{2,1,0:T(8,128)S(1)}, f32[2,5,128]{2,1,0:T(8,128)S(1)}, f32[128,2,5,128]{3,0,2,1:T(8,128)S(1)}, s32[128]{0:T(128)S(1)},...) while((s32[]{:T(128)}, f32[2,5,128]{2,1,0:T(8,128)S(1)}, ...), condition=%wide.region_12.13_spmd, body=%wide.region_5.12_spmd.sunk | while | flops 590231040 | bytes 6574921 | solution.py:135
  170.6 0.7 broadcast_compare_fusion.4
  172.1 0.7 broadcast_compare_fusion.4
  173.5 3.1 conditional.4
  173.5 1.0 constant_dynamic-slice_fusion
  175.2 1.4 fusion.2
  176.8 0.7 broadcast_compare_fusion.4
  178.3 0.7 broadcast_compare_fusion.4
  179.8 0.7 broadcast_compare_fusion.4
  181.4 0.7 broadcast_compare_fusion.4
  182.9 0.7 broadcast_compare_fusion.4
  184.4 0.7 broadcast_compare_fusion.4
  185.9 1.1 copy.150
  187.0 1.2 multiply_reduce_fusion
  188.2 0.5 fusion.26
  188.7 1.1 fusion.27
  189.8 1.3 copy.152
  191.1 1.6 broadcast.285
  192.7 1.6 broadcast.285.clone
  194.3 18.1 %while.39 = (s32[]{:T(128)}, f32[128,2,5,128]{3,0,2,1:T(8,128)S(1)}, f32[2048,256]{0,1:T(8,128)}, f32[2048,256]{0,1:T(8,128)}, s32[128]{0:T(128)S(1)}, /*index=5...) while((s32[]{:T(128)}, ...), condition=%wide.region_19.20_spmd, body=%wide.region_14.19_spmd.sunk | while | flops 422323968 | bytes 11615105 | solution.py:182
  194.4 0.7 broadcast_compare_fusion.5
  195.9 0.7 broadcast_compare_fusion.5
  197.3 5.9 %conditional.5 = ((f32[128,2,5,128]{3,0,2,1:T(8,128)S(1)}, f32[2048,256]{0,1:T(8,128)}, f32[2048,256]{0,1:T(8,128)})) conditional(s32[]{:T(128)} %convert_element_type.114, (f32[128,2,5,128]{3,0,2,1:T(8,128)S(1)}, f32[2048,256]{0,1:T(8,128)}, f32[2048,256]{0,1:T(8,128)}) %tuple.133, (pred[128,256]{0,1:T(8,128)(4,1)S(1)}, s32[]{:T(128)}, ...), branch_computations={%region_17.17_spmd, %region_18.18_spmd} | conditional | flops 422248448 | bytes 11577422 | solution.py:180
  197.4 0.9 constant_dynamic-slice_fusion.3
  198.7 0.9 constant_dynamic-slice_fusion.2
  200.1 0.5 fusion.18
  201.3 1.9 constant_dynamic-update-slice_fusion
  203.3 0.7 broadcast_compare_fusion.5
  204.8 0.7 broadcast_compare_fusion.5
  206.4 0.7 broadcast_compare_fusion.5
  207.9 0.7 broadcast_compare_fusion.5
  209.4 0.7 broadcast_compare_fusion.5
  211.0 0.7 broadcast_compare_fusion.5
  212.4 2.9 copy.162
  215.3 2.9 copy.163
  218.5 0.9 copy.155
  219.4 40.4 %all-gather.8.cloned.1.call-done = bf16[5120,1280]{1,0:T(8,128)(2,1)} async-done(((bf16[80,1280]{1,0:T(8,128)(2,1)}), bf16[5120,1280]{1,0:T(8,128)(2,1)}) %all-gather.8.cloned.1.call-update) | async-done | bytes 13107216 | tf_op jit(solution)/shard_map/all_gather | solution.py:198
  259.8 10.3 %convolution_convert_fusion = bf16[128,5120]{1,0:T(8,128)(2,1)} fusion(bf16[128,1280]{0,1:T(8,128)(2,1)} %bitcast.160, bf16[5120,1280]{1,0:T(8,128)(2,1)} %all-gather.8.cloned.1.call-done), kind=kOutput, calls=%fused_computation.52 | convolution fusion | flops 1678376960 | bytes 14745600 | tf_op jit(solution)/shard_map/dot_general | solution.py:196
  270.6 2.2 collective-permute-start.2
  273.2 0.9 copy.164
  274.4 1.9 collective-permute-start.3
  276.4 0.6 add_convert_fusion.1
  277.0 3.0 collective-permute-done.3
  280.0 0.6 add_convert_fusion
  280.7 115.4 %reduce-scatter.4.cloned.1.call-done = f32[32,256]{1,0:T(8,128)} async-done(((f32[2048,256]{1,0:T(8,128)}), f32[32,256]{1,0:T(8,128)}) %reduce-scatter.4.cloned.1.call-update) | async-done | bytes 32784 | tf_op jit(solution)/shard_map/reduce_scatter | solution.py:192
  396.0 1.4 convert_element_type.93
  397.4 141.8 %reduce-scatter.6.cloned.1.call-done = f32[32,256]{1,0:T(8,128)} async-done(((f32[2048,256]{1,0:T(8,128)}), f32[32,256]{1,0:T(8,128)}) %reduce-scatter.6.cloned.1.call-update) | async-done | bytes 32784 | tf_op jit(solution)/shard_map/reduce_scatter | solution.py:193
  539.2 1.4 convert_element_type.94
  540.5 31.3 %reduce-scatter.8.cloned.1.call-done = bf16[128,1280]{1,0:T(8,128)(2,1)} async-done(((bf16[128,5120]{1,0:T(8,128)(2,1)}), bf16[128,1280]{1,0:T(8,128)(2,1)}) %reduce-scatter.8.cloned.1.call-update) | async-done | bytes 327696 | tf_op jit(solution)/shard_map/reduce_scatter | solution.py:202
  (105 shorter events, 7.3 us)
Async XLA Ops:
  7.2 12.9 %copy-start.3 = (bf16[128,1280]{1,0:T(8,128)(2,1)S(1)}, bf16[128,1280]{1,0:T(8,128)(2,1)}, u32[]{:S(2)}) copy-start(bf16[128,1280]{1,0:T(8,128)(2,1)} %param.17) | copy-start | bytes 983044
  7.2 84.2 %all-gather.4.cloned.1.call-start = ((), (), s32[]{:S(2)}) async-start(), calls=%async_computation.3 | async-start | bytes 1064960 | tf_op jit(solution)/shard_map/all_gather | solution.py:113
  7.9 160.3 %all-gather.6.cloned.1.call-start = ((), (), s32[]{:S(2)}) async-start(), calls=%async_computation.4 | async-start | bytes 1064960 | tf_op jit(solution)/shard_map/all_gather | solution.py:114
  8.7 11.9 %copy-start.4 = (bf16[128,256]{1,0:T(8,128)(2,1)S(1)}, bf16[128,256]{1,0:T(8,128)(2,1)}, u32[]{:S(2)}) copy-start(bf16[128,256]{1,0:T(8,128)(2,1)} %param.19) | copy-start | bytes 196612
  8.7 251.1 %all-gather.8.cloned.1.call-start = ((), (), s32[]{:S(2)}) async-start(), calls=%async_computation.7 | async-start | bytes 13312000 | tf_op jit(solution)/shard_map/all_gather | solution.py:198
  9.4 386.6 %reduce-scatter.4.cloned.1.call-start = ((), (), s32[]{:S(2)}) async-start(), calls=%async_computation.5 | async-start | bytes 2129920 | tf_op jit(solution)/shard_map/reduce_scatter | solution.py:192
  10.4 10.3 %collective-permute-start = (bf16[128,256]{0,1:T(8,128)(2,1)S(1)}, bf16[128,256]{0,1:T(8,128)(2,1)S(1)}, u32[]{:S(2)}, u32[]{:S(2)}) collective-permute-start(bf16[128,256]{0,1:T(8,128)(2,1)S(1)} %copy.135), channel_id=1, source_target_pairs={{0,4},{4,8},{8,12},{12,16},{16,20},{20,24},{24,28},{28,32},{32,36}... | collective-permute-start | bytes 196616 | tf_op jit(solution)/shard_map/ppermute | solution.py:21
  14.9 5.6 collective-permute-start.1
  20.7 0.8 copy-start.1
  93.6 76.9 %copy-start.5 = (s32[8]{0:T(128)S(1)}, s32[8]{0:T(128)}, u32[]{:S(2)}) copy-start(s32[8]{0:T(128)} %param.25) | copy-start | bytes 100
  185.8 2.3 copy-start.2
  215.3 323.9 %reduce-scatter.6.cloned.1.call-start = ((), (), s32[]{:S(2)}) async-start(), calls=%async_computation.6 | async-start | bytes 2129920 | tf_op jit(solution)/shard_map/reduce_scatter | solution.py:193
  218.3 353.5 %reduce-scatter.8.cloned.1.call-start = ((), (), s32[]{:S(2)}) async-start(), calls=%async_computation.8 | async-start | bytes 1638400 | tf_op jit(solution)/shard_map/reduce_scatter | solution.py:202
  270.5 2.7 copy-start
  270.6 5.7 collective-permute-start.2
  274.4 5.6 collective-permute-start.3
Sparse Core Ops, SparseCore 0:
  10.8 80.5 all-gather.3
  94.1 74.0 all-gather.5
  170.9 88.7 all-gather.7
  263.7 132.3 reduce-scatter.3
  400.5 138.6 reduce-scatter.5
  542.2 29.6 reduce-scatter.7
where the time goes:
time: 580 us; the launch traced here: 579 us
  waiting for transfers between devices  475 us (82%)
  local copies, waits for them, and re-layouts  25.8 us (4%)
  other arithmetic  22.3 us (4%)
  matrix products  18.6 us (3%)
  between operations  14.5 us (2%)
  loops' own time  11.2 us (2%)
  starting transfers between devices  10.9 us (2%)
    reduce_scatter x1, waiting for transfers between devices, shards(): lax.psum_scatter(gpv, 'dp', scatter_dimension=0, tiled=True)  142 us
    reduce_scatter x1, waiting for transfers between devices, shards(): lax.psum_scatter(gpk, 'dp', scatter_dimension=0, tiled=True)  115 us
    all_gather x1, waiting for transfers between devices, shards(): lax.all_gather(prompt_slot_values, 'dp', axis=0, tiled=True)  74.6 us
    all_gather x1, waiting for transfers between devices, shards(): prompt_key_rows = lax.all_gather(prompt_slot_keys, 'dp', axis=0, tiled=True)  66.8 us
    all_gather x1, waiting for transfers between devices, shards(): lax.all_gather(query_weight, 'dp', axis=0, tiled=True)  40.4 us
    reduce_scatter x1, waiting for transfers between devices, shards(): lax.psum_scatter(partial_input.astype(jnp.bfloat16), 'tensor', scatter_di...  31.3 us
    eq x16, other arithmetic, step(): mask = rprompt[:, None] == kprompt[None, :]  11.8 us
  transfers between devices with their start and end apart: 10, of which 7 were waited for; matrix products, arithmetic and copies ran while one was open for 12% of the time, Pallas kernels for 0%

commit v1 on v0

v1 whole, which is shorter than its diff:
```python
import functools
import math

import jax
import jax.numpy as jnp
from jax import lax
from jax.experimental import pallas as pl
from jax.experimental.pallas import tpu as pltpu
from jax.sharding import PartitionSpec as P

QUERY_HEADS = 40
KEY_VALUE_HEADS = 8
GROUP = QUERY_HEADS // KEY_VALUE_HEADS
HEAD = 128
PROMPTS = 8
RESP_PER = 16
RESPONSES = 128
NZ, NX, NC, NY = 8, 4, 2, 4
TOK = 128
KVH = 2
PROWS = 32
WROWS = 80
QCOLS = KVH * GROUP * HEAD
LANES = GROUP * HEAD
BLK = NZ * WROWS // NY

NEG = -1e30
SCALE = 1.0 / math.sqrt(HEAD)
F32 = jnp.float32
BF = jnp.bfloat16
MESH = pl.DeviceIdType.MESH


def dot(a, b, ca, cb):
    return lax.dot_general(a, b, (((ca,), (cb,)), ((), ())), preferred_element_type=F32)


def kernel(
    near, wide, nsem,
    q_ref, k_ref, v_ref, g_ref, pk_ref, pv_ref, w_ref, lenv_ref, lens_ref, owner_ref,
    gq_ref, gk_ref, gv_ref, gpk_ref, gpv_ref, gi_ref,
    kvz, kvg, wk, wv, wall, gqall, qm, gm, sbuf, dbuf, pbuf, dsbuf, dsm,
    acc, accw, wsend, wrecv, csend, crecv, xown, xsend, xrecv, gsum, zsend, zrecv,
    part, ysend, yrecv, osend, ogi, send_sem, recv_sem,
):
    dp = lax.axis_index("dp")
    y = lax.axis_index("tensor")
    z, x, c = dp // 8, (dp // 2) % 4, dp % 2
    gidx = dp % 8
    oc = 1 - c

    def device(dz=0, dx=0, flip=False, dy=0):
        z2 = lax.rem(z + dz, NZ)
        x2 = lax.rem(x + dx, NX)
        c2 = oc if flip else c
        return (z2 * 8 + x2 * 2 + c2, lax.rem(y + dy, NY))

    nxt = (lax.rem(dp + 1, 64), y)
    prv = (lax.rem(dp + 63, 64), y)
    count = [0]

    def send(src, dst, target):
        i = count[0]
        count[0] = i + 1
        copy = pltpu.make_async_remote_copy(
            src_ref=src, dst_ref=dst, send_sem=send_sem.at[i], recv_sem=recv_sem.at[i],
            device_id=target, device_id_type=MESH,
        )
        copy.start()
        sent.append(copy)
        return copy

    sent = []
    barrier = pltpu.get_barrier_semaphore()
    peers = [device(dz=d) for d in range(1, NZ)]
    peers += [device(dx=d) for d in range(1, NX)]
    peers += [device(flip=True)]
    peers += [device(dy=d) for d in range(1, NY)]
    peers += [nxt, prv]
    for peer in peers:
        pl.semaphore_signal(barrier, inc=1, device_id=peer, device_id_type=MESH)

    kvz[pl.ds(z, 1), :, 0:256] = pk_ref[...][None]
    kvz[pl.ds(z, 1), :, 256:512] = pv_ref[...][None]
    wk[TOK:, :] = k_ref[...]
    wv[TOK:, :] = v_ref[...]
    wall[pl.ds(z, 1)] = w_ref[...][None]

    pl.semaphore_wait(barrier, len(peers))
    zin = [
        send(kvz.at[pl.ds(z, 1)], kvz.at[pl.ds(z, 1)], device(dz=d))
        for d in (4, 3, 5, 2, 6, 1, 7)
    ]
    nin = [
        send(k_ref, wk.at[pl.ds(0, TOK)], nxt),
        send(v_ref, wv.at[pl.ds(0, TOK)], nxt),
    ]

    first = dp * TOK
    ri = lax.broadcasted_iota(jnp.int32, (RESPONSES, RESPONSES), 0)
    ci = lax.broadcasted_iota(jnp.int32, (RESPONSES, RESPONSES), 1)
    len_l = jnp.broadcast_to(lenv_ref[...].astype(F32), (RESPONSES, RESPONSES))
    len_col = jnp.sum(jnp.where(ri == ci, len_l, 0.0), axis=1, keepdims=True)
    ends_col = jnp.sum(jnp.where(ci <= ri, len_l, 0.0), axis=1, keepdims=True)
    len_s = jnp.broadcast_to(len_col, (RESPONSES, RESPONSES))
    ends_row = jnp.sum(jnp.where(ri <= ci, len_s, 0.0), axis=0, keepdims=True)
    rows_l = (first + ci).astype(F32)
    rows_s = (first + ri).astype(F32)
    before_l = ends_col <= rows_l
    before_s = ends_row <= rows_s
    resp_row = jnp.sum(jnp.where(before_l, 1.0, 0.0), axis=0, keepdims=True)
    start_row = jnp.sum(jnp.where(before_l, len_s, 0.0), axis=0, keepdims=True)
    resp_col = jnp.sum(jnp.where(before_s, 1.0, 0.0), axis=1, keepdims=True)
    prompt_row = jnp.floor(resp_row * (1.0 / RESP_PER))
    prompt_col = jnp.floor(resp_col * (1.0 / RESP_PER))
    wpos = (first - TOK + lax.broadcasted_iota(jnp.int32, (2 * TOK, TOK), 0)).astype(F32)
    wmask = (wpos >= start_row) & (wpos <= rows_l[0:1])

    first_group = z * (8 * TOK)

    def walk(r, carry):
        end, ng, nd = carry
        end = end + lens_ref[r]
        ng = ng + jnp.where(end <= first_group, 1, 0)
        nd = nd + jnp.where(end <= first, 1, 0)
        return (end, ng, nd)

    zero = jnp.int32(0)
    _, ng, nd = lax.fori_loop(0, RESPONSES, walk, (zero, zero, zero), unroll=8)
    pg = ng // RESP_PER
    pd = nd // RESP_PER
    slot_of = [owner_ref[jnp.minimum(pg + n, PROMPTS - 1)] for n in range(wide)]
    in_group = [jnp.minimum(pd - pg + n, wide - 1) for n in range(near)]

    mcol = [
        jnp.broadcast_to(jnp.where(prompt_col == (pd + n).astype(F32), 1.0, 0.0), (TOK, HEAD)).astype(BF)
        for n in range(near)
    ]
    mrow = [
        jnp.broadcast_to(jnp.where(prompt_row == (pd + n).astype(F32), 1.0, 0.0), (2 * TOK, TOK)).astype(BF)
        for n in range(near)
    ]
    for h in range(KVH):
        for g in range(GROUP):
            cols = slice((h * GROUP + g) * HEAD, (h * GROUP + g + 1) * HEAD)
            rows = slice(g * HEAD, (g + 1) * HEAD)
            qb = q_ref[:, cols]
            gb = g_ref[:, cols]
            qm[h, rows, near * HEAD:] = qb
            gm[h, rows, near * HEAD:] = gb
            for n in range(near):
                qm[h, rows, n * HEAD:(n + 1) * HEAD] = qb * mcol[n]
                gm[h, rows, n * HEAD:(n + 1) * HEAD] = gb * mcol[n]

    for copy in zin:
        copy.wait_recv()
    for n in range(wide):
        kvg[pl.ds(gidx, 1), n] = kvz[pl.ds(slot_of[n], 1)]
    own = kvg.at[pl.ds(gidx, 1)]
    xin = [send(own, own, device(dx=d)) for d in (1, 3, 2)]
    fin = [send(own, own, device(flip=True))]

    def ring(step):
        up = lax.rem(z + NZ - step, NZ)
        down = lax.rem(z + step, NZ)
        out = [send(wall.at[pl.ds(up, 1)], wall.at[pl.ds(up, 1)], device(dz=1))]
        if step < 3:
            out.append(send(wall.at[pl.ds(down, 1)], wall.at[pl.ds(down, 1)], device(dz=7)))
        return out

    win = ring(0)

    for copy in nin:
        copy.wait_recv()
    for h in range(KVH):
        hc = slice(h * HEAD, (h + 1) * HEAD)
        sbuf[h, 256:, :] = dot(wk[:, hc], qm[h, :, near * HEAD:], 1, 1)
        dbuf[h, 256:, :] = dot(wv[:, hc], gm[h, :, near * HEAD:], 1, 1)

    for d, copy in zip((1, 3, 2), xin):
        copy.wait_recv()
        block = kvg.at[pl.ds(lax.rem(x + NX - d, NX) * 2 + c, 1)]
        fin.append(send(block, block, device(flip=True)))
    for copy in win:
        copy.wait_recv()
    win = ring(1)
    for copy in fin:
        copy.wait_recv()

    def prompt_block(n, lo, width):
        block = kvg[:, pl.ds(in_group[n], 1), :, lo:lo + width]
        return block.reshape(8 * PROWS, width)

    acc[near] = jnp.zeros(acc.shape[1:], F32)
    gin = []
    for h in range(KVH):
        hc = slice(h * HEAD, (h + 1) * HEAD)
        kp = [prompt_block(n, h * HEAD, HEAD) for n in range(near)]
        vp = [prompt_block(n, 256 + h * HEAD, HEAD) for n in range(near)]
        sbuf[h, 0:256, :] = dot(jnp.concatenate(kp, axis=1), qm[h, :, 0:near * HEAD], 1, 1)
        dbuf[h, 0:256, :] = dot(jnp.concatenate(vp, axis=1), gm[h, :, 0:near * HEAD], 1, 1)
        for g in range(GROUP):
            gl = slice(g * HEAD, (g + 1) * HEAD)
            sp = sbuf[h, 0:256, gl] * SCALE
            sw = jnp.where(wmask, sbuf[h, 256:512, gl] * SCALE, NEG)
            high = jnp.maximum(
                jnp.max(sp, axis=0, keepdims=True), jnp.max(sw, axis=0, keepdims=True)
            )
            ep = jnp.exp(sp - high)
            ew = jnp.exp(sw - high)
            total = jnp.sum(ep, axis=0, keepdims=True) + jnp.sum(ew, axis=0, keepdims=True)
            inv = 1.0 / total
            pp = ep * inv
            pw = ew * inv
            dpp = dbuf[h, 0:256, gl]
            dpw = dbuf[h, 256:512, gl]
            delta = jnp.sum(pp * dpp, axis=0, keepdims=True) + jnp.sum(pw * dpw, axis=0, keepdims=True)
            dsp = (pp * (dpp - delta)).astype(BF)
            dsw = (pw * (dpw - delta)).astype(BF)
            pbuf[0:256, gl] = pp.astype(BF)
            pbuf[256:512, gl] = pw.astype(BF)
            dsbuf[:, gl] = dsp
            dsm[near * 256:, gl] = dsw
            for n in range(near):
                dsm[n * 256:(n + 1) * 256, gl] = dsp * mrow[n]
        keys = jnp.concatenate(kp + [wk[:, hc]], axis=0)
        dqt = (dot(keys, dsm[...], 0, 0) * SCALE)
        gqt = dqt.astype(BF)
        for g in range(GROUP):
            head = h * GROUP + g
            gl = slice(g * HEAD, (g + 1) * HEAD)
            gqall[0, 0, head * HEAD:(head + 1) * HEAD, :] = gqt[:, gl]
        half = pl.ds(h * LANES, LANES)
        mine = gqall.at[0, 0, half]
        gin.append(
            [send(mine, gqall.at[d, 0, half], device(dx=d)) for d in (1, 3, 2)]
            + [send(mine, gqall.at[0, 1, half], device(flip=True))]
        )
        for g in range(GROUP):
            head = h * GROUP + g
            gq_ref[:, head * HEAD:(head + 1) * HEAD] = dqt[:, g * HEAD:(g + 1) * HEAD].T.astype(BF)
        dv = dot(pbuf[0:256, :], gm[h, :, 0:near * HEAD], 1, 0)
        dk = dot(dsbuf[...], qm[h, :, 0:near * HEAD], 1, 0) * SCALE
        for n in range(near):
            acc[n, :, hc] = dk[:, n * HEAD:(n + 1) * HEAD]
            acc[n, :, 256 + h * HEAD:256 + (h + 1) * HEAD] = dv[:, n * HEAD:(n + 1) * HEAD]
        accw[0, :, hc] = dot(dsm[near * 256:, :], qm[h, :, near * HEAD:], 1, 0) * SCALE
        accw[1, :, hc] = dot(pbuf[256:512, :], gm[h, :, near * HEAD:], 1, 0)
        for copy in win:
            copy.wait_recv()
        win = ring(2 + h)

    wsend[...] = accw[:, 0:TOK, :].astype(BF)
    back = send(wsend, wrecv, prv)

    held = [
        jnp.where((pg + n - pd >= 0) & (pg + n - pd < near), pg + n - pd, near) for n in range(wide)
    ]

    def term(n, row):
        return acc[pl.ds(held[n], 1), pl.ds(pl.multiple_of(row * PROWS, PROWS), PROWS), :]

    for xs in range(NX):
        for n in range(wide):
            csend[xs, n:n + 1] = term(n, xs * 2 + oc).astype(BF)
    cin = send(csend, crecv, device(flip=True))

    def chunk(d):
        both = jnp.concatenate([gqall[d, 0], gqall[d, 1]], axis=1)
        part[d] = dot(wall[...].reshape(NZ * WROWS, QCOLS), both, 1, 0)
        ysend[d] = part[d].astype(BF)
        out = []
        for e in (2, 1, 3):
            rows = pl.ds(pl.multiple_of(lax.rem(y + e, NY) * BLK, 16), BLK)
            out.append(send(ysend.at[d, rows], yrecv.at[d, e - 1], device(dy=e)))
        return out

    def finish(d, copies):
        for copy in copies:
            copy.wait_recv()
        total = part[d, pl.ds(pl.multiple_of(y * BLK, 16), BLK), :]
        for e in range(3):
            total = total + yrecv[d, e].astype(F32)
        total = total.astype(BF)
        osend[d, 0] = total[:, 0:TOK]
        osend[d, 1] = total[:, TOK:]
        target = lax.rem(x + NX - d, NX)
        out = []
        if d == 0:
            ogi[pl.ds(gidx, 1)] = total[:, 0:TOK][None]
        else:
            out.append(send(osend.at[d, pl.ds(0, 1)], ogi.at[pl.ds(gidx, 1)], (z * 8 + target * 2 + c, y)))
        out.append(send(osend.at[d, pl.ds(1, 1)], ogi.at[pl.ds(gidx, 1)], (z * 8 + target * 2 + oc, y)))
        return out

    for copy in win:
        copy.wait_recv()
    for copies in gin:
        copies[3].wait_recv()
    yin = {0: chunk(0)}

    cin.wait_recv()
    for n in range(wide):
        for xs in range(NX):
            total = term(n, xs * 2 + c) + crecv[xs, n:n + 1].astype(F32)
            xown[xs, n:n + 1] = total
            xsend[xs, n:n + 1] = total.astype(BF)
    rin = [
        send(xsend.at[lax.rem(x + d, NX)], xrecv.at[d - 1], device(dx=d)) for d in (1, 3, 2)
    ]

    oin = []
    forwarded = {}
    for i, d in ((0, 1), (1, 3), (2, 2)):
        forwarded[d] = []
        for h in range(KVH):
            half = pl.ds(h * LANES, LANES)
            gin[h][i].wait_recv()
            forwarded[d].append(send(gqall.at[d, 0, half], gqall.at[d, 1, half], device(flip=True)))
        for copy in forwarded[d]:
            copy.wait_recv()
        yin[d] = chunk(d)
        if d == 1:
            oin += finish(0, yin[0])
        elif d == 3:
            for copy in rin:
                copy.wait_recv()
            for n in range(wide):
                total = xown[pl.ds(x, 1), n:n + 1][0]
                for e in range(3):
                    total = total + xrecv[e, n:n + 1].astype(F32)
                gsum[n:n + 1] = total
            gsum[wide] = jnp.zeros(gsum.shape[1:], F32)

            def pick(target):
                index = jnp.int32(wide)
                for n in range(wide):
                    hit = (slot_of[n] == target) & (pg + n < PROMPTS)
                    index = jnp.where(hit, n, index)
                return gsum[pl.ds(index, 1)]

            gin_z = []
            for dz in (4, 3, 5, 2, 6, 1, 7):
                zsend[dz - 1:dz] = pick(lax.rem(z + dz, NZ)).astype(BF)
                gin_z.append(send(zsend.at[dz - 1], zrecv.at[dz - 1], device(dz=dz)))
            oin += finish(1, yin[1])
        else:
            oin += finish(3, yin[3])
    oin += finish(2, yin[2])

    back.wait_recv()
    gk_ref[...] = (accw[0, TOK:, :] + wrecv[0].astype(F32)).astype(BF)
    gv_ref[...] = (accw[1, TOK:, :] + wrecv[1].astype(F32)).astype(BF)
    for copy in gin_z:
        copy.wait_recv()
    total = pick(z)[0]
    for e in range(NZ - 1):
        total = total + zrecv[e].astype(F32)
    gpk_ref[...] = total[:, 0:256].astype(BF)
    gpv_ref[...] = total[:, 256:512].astype(BF)

    for copy in oin:
        copy.wait_recv()
    blocks = []
    for zz in range(2):
        for j in range(8):
            blocks.append(ogi[j, zz * WROWS:(zz + 1) * WROWS, :])
    git = jnp.concatenate(blocks, axis=0)
    for i in range(QCOLS // HEAD):
        gi_ref[:, i * HEAD:(i + 1) * HEAD] = git[i * HEAD:(i + 1) * HEAD, :].astype(F32).T.astype(BF)
    for copy in sent:
        copy.wait_send()
    assert count[0] <= nsem


def fused(near, wide, cid, queries, keys, values, output_gradient, pk, pv, weight, lengths, owner):
    nsem = 72
    vm = pl.BlockSpec(memory_space=pltpu.VMEM)
    sm = pl.BlockSpec(memory_space=pltpu.SMEM)
    shape = jax.ShapeDtypeStruct
    scratch = [
        pltpu.VMEM((NZ, PROWS, 512), BF),
        pltpu.VMEM((8, wide, PROWS, 512), BF),
        pltpu.VMEM((2 * TOK, 256), BF),
        pltpu.VMEM((2 * TOK, 256), BF),
        pltpu.VMEM((NZ, WROWS, QCOLS), BF),
        pltpu.VMEM((NX, 2, QCOLS, TOK), BF),
        pltpu.VMEM((KVH, LANES, (near + 1) * HEAD), BF),
        pltpu.VMEM((KVH, LANES, (near + 1) * HEAD), BF),
        pltpu.VMEM((KVH, 512, LANES), F32),
        pltpu.VMEM((KVH, 512, LANES), F32),
        pltpu.VMEM((512, LANES), BF),
        pltpu.VMEM((256, LANES), BF),
        pltpu.VMEM(((near + 1) * 256, LANES), BF),
        pltpu.VMEM((near + 1, 256, 512), F32),
        pltpu.VMEM((2, 2 * TOK, 256), F32),
        pltpu.VMEM((2, TOK, 256), BF),
        pltpu.VMEM((2, TOK, 256), BF),
        pltpu.VMEM((NX, wide, PROWS, 512), BF),
        pltpu.VMEM((NX, wide, PROWS, 512), BF),
        pltpu.VMEM((NX, wide, PROWS, 512), F32),
        pltpu.VMEM((NX, wide, PROWS, 512), BF),
        pltpu.VMEM((NX - 1, wide, PROWS, 512), BF),
        pltpu.VMEM((wide + 1, PROWS, 512), F32),
        pltpu.VMEM((NZ - 1, PROWS, 512), BF),
        pltpu.VMEM((NZ - 1, PROWS, 512), BF),
        pltpu.VMEM((NX, NZ * WROWS, 2 * TOK), F32),
        pltpu.VMEM((NX, NZ * WROWS, 2 * TOK), BF),
        pltpu.VMEM((NX, NY - 1, BLK, 2 * TOK), BF),
        pltpu.VMEM((NX, 2, BLK, TOK), BF),
        pltpu.VMEM((8, BLK, TOK), BF),
        pltpu.SemaphoreType.DMA((nsem,)),
        pltpu.SemaphoreType.DMA((nsem,)),
    ]
    return pl.pallas_call(
        functools.partial(kernel, near, wide, nsem),
        out_shape=(
            shape((TOK, QCOLS), BF),
            shape((TOK, 256), BF),
            shape((TOK, 256), BF),
            shape((PROWS, 256), BF),
            shape((PROWS, 256), BF),
            shape((TOK, QCOLS), BF),
        ),
        in_specs=[vm] * 8 + [sm] * 2,
        out_specs=(vm,) * 6,
        scratch_shapes=scratch,
        compiler_params=pltpu.CompilerParams(
            collective_id=cid, has_side_effects=True, vmem_limit_bytes=56 * 2**20
        ),
    )(
        queries, keys, values, output_gradient, pk, pv, weight,
        lengths.reshape(1, RESPONSES), lengths, owner,
    )


NEARWIDE = (6, 6)


def shards(*args):
    return fused(*NEARWIDE, 0, *args)


def solution(mesh):
    split = P("dp", "tensor")
    return jax.shard_map(
        shards,
        mesh=mesh,
        in_specs=(split,) * 7 + (P(), P()),
        out_specs=(split,) * 6,
        check_vma=False,
    )
```

time: 580 us -> 79.3 us (0.14)
  waiting for transfers between devices: 475 us -> 0 us
  Pallas kernels: 0 us -> 72 us
  other arithmetic: 22.3 us -> 0 us
  local copies, waits for them, and re-layouts: 25.8 us -> 5.41 us
  matrix products: 18.6 us -> 0 us
  between operations: 14.5 us -> 0.67 us
  loops' own time: 11.2 us -> 0 us
  starting transfers between devices: 10.9 us -> 0 us
    reduce_scatter x3 -> x0, waiting for transfers between devices: 288 us -> none  [the longest x1 142 us: shards(): lax.psum_scatter(gpv, 'dp', scatter_dimension=0, tiled=True)]
    all_gather x3 -> x0, waiting for transfers between devices: 182 us -> none  [the longest x1 74.6 us: shards(): lax.all_gather(prompt_slot_values, 'dp', axis=0, tiled=True)]
    pallas_call x0 -> x1, Pallas kernels: none -> 72 us  [fused(): pl.pallas_call(functools.partial(kernel, near, wide, nsem), out_shape=(sh...]
    dot_general x14 -> x0, matrix products: 18.6 us -> none  [the longest x1 10.3 us: shards(): lax.dot_general(grad_queries, lax.all_gather(query_weight, 'dp', axis=0,...]
    while x9 -> x0, local copies, waits for them, and re-layouts: 15.2 us -> none  [the longest x4 8.02 us: shards(): dquery, gpk, gpv = lax.fori_loop(0, size // prompt_width, step, binit)]
    eq x16 -> x0, other arithmetic: 11.8 us -> none  [step(): mask = rprompt[:, None] == kprompt[None, :]]
    another operation x18 -> x0, loops' own time: 11.2 us -> none  [the longest x1 5.46 us: shards(): state = lax.fori_loop(0, size // width, step, state)]
    ppermute x4 -> x0, starting transfers between devices: 10.5 us -> none  [from_behind(): lax.ppermute(value, axis, [(source, source + steps) for source in range(f...]
  transfers between devices with their start and end apart: 10 -> 0, of which waited for: 7 -> 0; matrix products, arithmetic and copies ran while one was open for 12% -> 0% of each run, Pallas kernels for 0% -> 0%
where the time goes in v1:
time: 79.3 us; the launch traced here: 78 us
  Pallas kernels  72 us (91%)
  local copies, waits for them, and re-layouts  5.41 us (7%)
    pallas_call x1, Pallas kernels, fused(): pl.pallas_call(functools.partial(kernel, near, wide, nsem), out_shape=(sh...  72 us
    unnamed x16, local copies, waits for them, and re-layouts  5.41 us

profile of v1, /device:TPU:1, one launch (start us, length us, event | category | flops | bytes accessed | tf_op | source)
XLA Modules:
  0.0 78.0 jit_solution(4445358475468177540)
XLA Ops:
  0.6 72.0 %shard_map.136 = (bf16[128,1280]{1,0:T(8,128)(2,1)}, bf16[128,256]{1,0:T(8,128)(2,1)}, bf16[128,256]{1,0:T(8,128)(2,1)}, bf16[32,256]{1,0:T(8,128)(2,1)}, bf16[3...) custom-call(bf16[128,1280]{1,0:T(8,128)(2,1)} %q_ref.1, bf16[128,256]{1,0:T(8,128)(2,1)} %k_ref.1, bf16[128,256]{1,0:T(8,128)(2,1)} %v_ref.1, ...), custom_call_target="tpu_custom_call" | custom-call | tf_op jit(solution)/shard_map/pallas_call | solution.py:415
  72.6 0.0 copy-start.2
  72.6 0.0 copy-start
  72.6 1.8 %copy.21 = bf16[128,1280]{1,0:T(8,128)(2,1)} copy(bf16[128,1280]{1,0:T(8,128)(2,1)} %get-tuple-element.12) | data formatting | bytes 655360
  74.4 0.0 copy-done.2
  74.4 0.0 copy-start.1
  74.4 0.6 copy.22
  75.0 0.2 copy-done.1
  75.3 0.0 copy-start.4
  75.3 0.6 copy.23
  75.9 0.1 copy-done.4
  76.0 0.0 copy-start.3
  76.0 0.6 copy.24
  76.6 0.1 copy-done.3
  76.7 0.6 copy.25
  77.3 0.0 copy-done
  77.3 0.7 copy.26
Async XLA Ops:
  72.6 1.8 %copy-start.2 = (bf16[128,256]{1,0:T(8,128)(2,1)S(1)}, bf16[128,256]{1,0:T(8,128)(2,1)}, u32[]{:S(2)}) copy-start(bf16[128,256]{1,0:T(8,128)(2,1)} %get-tuple-element.13) | copy-start | bytes 196612
  72.6 4.7 %copy-start = (bf16[128,1280]{1,0:T(8,128)(2,1)S(1)}, bf16[128,1280]{1,0:T(8,128)(2,1)}, u32[]{:S(2)}) copy-start(bf16[128,1280]{1,0:T(8,128)(2,1)} %get-tuple-element.17) | copy-start | bytes 983044
  74.4 0.9 %copy-start.1 = (bf16[128,256]{1,0:T(8,128)(2,1)S(1)}, bf16[128,256]{1,0:T(8,128)(2,1)}, u32[]{:S(2)}) copy-start(bf16[128,256]{1,0:T(8,128)(2,1)} %get-tuple-element.14) | copy-start | bytes 196612
  75.3 0.7 copy-start.4
  76.0 0.7 copy-start.3

commit v2 on v1

v2 whole, which is shorter than its diff:
```python
import functools
import math

import jax
import jax.numpy as jnp
from jax import lax
from jax.experimental import pallas as pl
from jax.experimental.pallas import tpu as pltpu
from jax.sharding import PartitionSpec as P

QUERY_HEADS = 40
KEY_VALUE_HEADS = 8
GROUP = QUERY_HEADS // KEY_VALUE_HEADS
HEAD = 128
PROMPTS = 8
RESP_PER = 16
RESPONSES = 128
NZ, NX, NC, NY = 8, 4, 2, 4
TOK = 128
KVH = 2
PROWS = 32
WROWS = 80
QCOLS = KVH * GROUP * HEAD
LANES = GROUP * HEAD
BLK = NZ * WROWS // NY

NEG = -1e30
SCALE = 1.0 / math.sqrt(HEAD)
F32 = jnp.float32
BF = jnp.bfloat16
MESH = pl.DeviceIdType.MESH


def dot(a, b, ca, cb):
    return lax.dot_general(a, b, (((ca,), (cb,)), ((), ())), preferred_element_type=F32)


def kernel(
    near, wide, nsem,
    q_hbm, k_hbm, v_hbm, g_hbm, pk_hbm, pv_hbm, w_hbm, lenv_ref, lens_ref, owner_ref,
    gq_hbm, gk_hbm, gv_hbm, gpk_hbm, gpv_hbm, gi_hbm,
    q_ref, g_ref, gq_ref, gk_ref, gv_ref, gpk_ref, gpv_ref, gi_ref,
    kz, vz, kg, vg, wk, wv, wall, gqall, qm, gm, sbuf, dbuf, pbuf, dsbuf, dsm,
    acc, accw, wsend, wrecv, csend, crecv, xown, xsend, xrecv, gsum, zsend, zrecv,
    part, ysend, ycomb, yrecv, osend, ogi, send_sem, recv_sem, local_sem,
):
    dp = lax.axis_index("dp")
    y = lax.axis_index("tensor")
    z, x, c = dp // 8, (dp // 2) % 4, dp % 2
    gidx = dp % 8
    oc = 1 - c

    def device(dz=0, dx=0, flip=False, dy=0):
        z2 = lax.rem(z + dz, NZ)
        x2 = lax.rem(x + dx, NX)
        c2 = oc if flip else c
        return (z2 * 8 + x2 * 2 + c2, lax.rem(y + dy, NY))

    nxt = (lax.rem(dp + 1, 64), y)
    prv = (lax.rem(dp + 63, 64), y)
    count = [0]
    sent = []
    stores = []

    def send(src, dst, target):
        i = count[0]
        count[0] = i + 1
        copy = pltpu.make_async_remote_copy(
            src_ref=src, dst_ref=dst, send_sem=send_sem.at[i], recv_sem=recv_sem.at[i],
            device_id=target, device_id_type=MESH,
        )
        copy.start()
        sent.append(copy)
        return copy

    def store(src, dst):
        copy = pltpu.make_async_copy(src, dst, local_sem.at[7 + len(stores)])
        copy.start()
        stores.append(copy)

    def arrive(copies):
        for copy in copies:
            copy.wait_recv()

    barrier = pltpu.get_barrier_semaphore()
    peers = [device(dz=d) for d in range(1, NZ)]
    peers += [device(dx=d) for d in range(1, NX)]
    peers += [device(flip=True)]
    peers += [device(dy=d) for d in range(1, NY)]
    peers += [nxt, prv]
    for peer in peers:
        pl.semaphore_signal(barrier, inc=1, device_id=peer, device_id_type=MESH)

    loads = [
        pltpu.make_async_copy(src, dst, local_sem.at[i])
        for i, (src, dst) in enumerate([
            (pk_hbm, kz.at[z]),
            (pv_hbm, vz.at[z]),
            (k_hbm, wk.at[pl.ds(TOK, TOK)]),
            (v_hbm, wv.at[pl.ds(TOK, TOK)]),
            (w_hbm, wall.at[z]),
            (q_hbm, q_ref),
            (g_hbm, g_ref),
        ])
    ]
    for load in loads:
        load.start()
    for load in loads[:4]:
        load.wait()
    pl.semaphore_wait(barrier, len(peers))
    far = (4, 3, 5, 2, 6, 1, 7)
    zk_in = [send(kz.at[z], kz.at[z], device(dz=d)) for d in far]
    zv_in = [send(vz.at[z], vz.at[z], device(dz=d)) for d in far]
    near_in = [
        send(wk.at[pl.ds(TOK, TOK)], wk.at[pl.ds(0, TOK)], nxt),
        send(wv.at[pl.ds(TOK, TOK)], wv.at[pl.ds(0, TOK)], nxt),
    ]

    first = dp * TOK
    ri = lax.broadcasted_iota(jnp.int32, (RESPONSES, RESPONSES), 0)
    ci = lax.broadcasted_iota(jnp.int32, (RESPONSES, RESPONSES), 1)
    len_l = jnp.broadcast_to(lenv_ref[...].astype(F32), (RESPONSES, RESPONSES))
    len_col = jnp.sum(jnp.where(ri == ci, len_l, 0.0), axis=1, keepdims=True)
    ends_col = jnp.sum(jnp.where(ci <= ri, len_l, 0.0), axis=1, keepdims=True)
    len_s = jnp.broadcast_to(len_col, (RESPONSES, RESPONSES))
    ends_row = jnp.sum(jnp.where(ri <= ci, len_s, 0.0), axis=0, keepdims=True)
    rows_l = (first + ci).astype(F32)
    rows_s = (first + ri).astype(F32)
    before_l = ends_col <= rows_l
    before_s = ends_row <= rows_s
    resp_row = jnp.sum(jnp.where(before_l, 1.0, 0.0), axis=0, keepdims=True)
    start_row = jnp.sum(jnp.where(before_l, len_s, 0.0), axis=0, keepdims=True)
    resp_col = jnp.sum(jnp.where(before_s, 1.0, 0.0), axis=1, keepdims=True)
    prompt_row = jnp.floor(resp_row * (1.0 / RESP_PER))
    prompt_col = jnp.floor(resp_col * (1.0 / RESP_PER))
    wpos = (first - TOK + lax.broadcasted_iota(jnp.int32, (2 * TOK, TOK), 0)).astype(F32)
    wmask = (wpos >= start_row) & (wpos <= rows_l[0:1])

    first_group = z * (8 * TOK)

    def walk(r, carry):
        end, ng, nd = carry
        end = end + lens_ref[r]
        ng = ng + jnp.where(end <= first_group, 1, 0)
        nd = nd + jnp.where(end <= first, 1, 0)
        return (end, ng, nd)

    zero = jnp.int32(0)
    _, ng, nd = lax.fori_loop(0, RESPONSES, walk, (zero, zero, zero), unroll=8)
    pg = ng // RESP_PER
    pd = nd // RESP_PER
    slot_of = [owner_ref[jnp.minimum(pg + n, PROMPTS - 1)] for n in range(wide)]
    in_group = [jnp.minimum(pd - pg + n, wide - 1) for n in range(near)]
    held = [
        jnp.where((pg + n - pd >= 0) & (pg + n - pd < near), pg + n - pd, near) for n in range(wide)
    ]

    mcol = [
        jnp.broadcast_to(jnp.where(prompt_col == (pd + n).astype(F32), 1.0, 0.0), (TOK, HEAD)).astype(BF)
        for n in range(near)
    ]
    mrow = [
        jnp.broadcast_to(jnp.where(prompt_row == (pd + n).astype(F32), 1.0, 0.0), (2 * TOK, TOK)).astype(BF)
        for n in range(near)
    ]
    for load in loads[4:]:
        load.wait()
    for h in range(KVH):
        for g in range(GROUP):
            cols = slice((h * GROUP + g) * HEAD, (h * GROUP + g + 1) * HEAD)
            rows = slice(g * HEAD, (g + 1) * HEAD)
            qb = q_ref[:, cols]
            gb = g_ref[:, cols]
            qm[h, rows, near * HEAD:] = qb
            gm[h, rows, near * HEAD:] = gb
            for n in range(near):
                qm[h, rows, n * HEAD:(n + 1) * HEAD] = qb * mcol[n]
                gm[h, rows, n * HEAD:(n + 1) * HEAD] = gb * mcol[n]

    def spread(source, dest):
        for n in range(wide):
            dest[pl.ds(gidx, 1), n] = source[pl.ds(slot_of[n], 1)]
        own = dest.at[pl.ds(gidx, 1)]
        across = [send(own, own, device(dx=d)) for d in (1, 3, 2)]
        return across, [send(own, own, device(flip=True))]

    def collect(dest, across, flips):
        for d, copy in zip((1, 3, 2), across):
            copy.wait_recv()
            block = dest.at[pl.ds(lax.rem(x + NX - d, NX) * 2 + c, 1)]
            flips.append(send(block, block, device(flip=True)))
        arrive(flips)

    arrive(zk_in)
    kx_in, kf_in = spread(kz, kg)
    arrive(zv_in)
    vx_in, vf_in = spread(vz, vg)

    pieces = (pl.ds(0, 48), pl.ds(48, 32))

    def ring(step, piece):
        up = wall.at[lax.rem(z + NZ - step, NZ), pieces[piece]]
        down = wall.at[lax.rem(z + step, NZ), pieces[piece]]
        if step == 3:
            return [send(up, up, device(dz=1))] if piece == 0 else [send(down, down, device(dz=7))]
        return [send(up, up, device(dz=1)), send(down, down, device(dz=7))]

    ring_in = {}

    def advance(step, piece):
        if step > 0:
            arrive(ring_in[step - 1, piece])
        ring_in[step, piece] = ring(step, piece)

    advance(0, 0)
    advance(0, 1)

    arrive(near_in)
    for h in range(KVH):
        hc = slice(h * HEAD, (h + 1) * HEAD)
        sbuf[h, 256:, :] = dot(wk[:, hc], qm[h, :, near * HEAD:], 1, 1)
        dbuf[h, 256:, :] = dot(wv[:, hc], gm[h, :, near * HEAD:], 1, 1)

    def prompt_block(source, n, h):
        block = source[:, pl.ds(in_group[n], 1), :, h * HEAD:(h + 1) * HEAD]
        return block.reshape(8 * PROWS, HEAD)

    collect(kg, kx_in, kf_in)
    kp = [[prompt_block(kg, n, h) for n in range(near)] for h in range(KVH)]
    for h in range(KVH):
        sbuf[h, 0:256, :] = dot(jnp.concatenate(kp[h], axis=1), qm[h, :, 0:near * HEAD], 1, 1)
    collect(vg, vx_in, vf_in)
    advance(1, 0)

    acc[near] = jnp.zeros(acc.shape[1:], F32)

    def softmax(h):
        vp = [prompt_block(vg, n, h) for n in range(near)]
        dbuf[h, 0:256, :] = dot(jnp.concatenate(vp, axis=1), gm[h, :, 0:near * HEAD], 1, 1)
        for g in range(GROUP):
            gl = slice(g * HEAD, (g + 1) * HEAD)
            sp = sbuf[h, 0:256, gl] * SCALE
            sw = jnp.where(wmask, sbuf[h, 256:512, gl] * SCALE, NEG)
            high = jnp.maximum(
                jnp.max(sp, axis=0, keepdims=True), jnp.max(sw, axis=0, keepdims=True)
            )
            ep = jnp.exp(sp - high)
            ew = jnp.exp(sw - high)
            total = jnp.sum(ep, axis=0, keepdims=True) + jnp.sum(ew, axis=0, keepdims=True)
            inv = 1.0 / total
            pp = ep * inv
            pw = ew * inv
            dpp = dbuf[h, 0:256, gl]
            dpw = dbuf[h, 256:512, gl]
            delta = jnp.sum(pp * dpp, axis=0, keepdims=True) + jnp.sum(pw * dpw, axis=0, keepdims=True)
            dsp = (pp * (dpp - delta)).astype(BF)
            dsw = (pw * (dpw - delta)).astype(BF)
            pbuf[0:256, gl] = pp.astype(BF)
            pbuf[256:512, gl] = pw.astype(BF)
            dsbuf[:, gl] = dsp
            dsm[near * 256:, gl] = dsw
            for n in range(near):
                dsm[n * 256:(n + 1) * 256, gl] = dsp * mrow[n]

    halves = [pl.ds(h * LANES, LANES) for h in range(KVH)]

    def query_grad(h):
        hc = slice(h * HEAD, (h + 1) * HEAD)
        keys = jnp.concatenate(kp[h] + [wk[:, hc]], axis=0)
        dqt = dot(keys, dsm[...], 0, 0) * SCALE
        gqt = dqt.astype(BF)
        for g in range(GROUP):
            head = h * GROUP + g
            gqall[0, 0, head * HEAD:(head + 1) * HEAD, :] = gqt[:, g * HEAD:(g + 1) * HEAD]
        mine = gqall.at[0, 0, halves[h]]
        copies = {d: send(mine, gqall.at[d, 0, halves[h]], device(dx=d)) for d in (1, 3)}
        copies[0] = send(mine, gqall.at[0, 1, halves[h]], device(flip=True))
        for g in range(GROUP):
            head = h * GROUP + g
            gq_ref[:, head * HEAD:(head + 1) * HEAD] = dqt[:, g * HEAD:(g + 1) * HEAD].T.astype(BF)
        return copies

    def pass_on(h, copies):
        out = []
        for d, lo in ((1, h * LANES), (3, h * LANES + LANES // 2)):
            copies[d].wait_recv()
            rows = pl.ds(lo, LANES // 2)
            out.append(send(gqall.at[d, 0, rows], gqall.at[2, 0, rows], device(dx=d)))
        flips = {
            d: send(gqall.at[d, 0, halves[h]], gqall.at[d, 1, halves[h]], device(flip=True))
            for d in (1, 3)
        }
        return out, flips

    def key_grad(h):
        hc = slice(h * HEAD, (h + 1) * HEAD)
        dv = dot(pbuf[0:256, :], gm[h, :, 0:near * HEAD], 1, 0)
        dk = dot(dsbuf[...], qm[h, :, 0:near * HEAD], 1, 0) * SCALE
        for n in range(near):
            acc[n, h, :, 0:HEAD] = dk[:, n * HEAD:(n + 1) * HEAD]
            acc[n, h, :, HEAD:] = dv[:, n * HEAD:(n + 1) * HEAD]
        for xs in range(NX):
            for n in range(wide):
                csend[h, xs, n] = term(h, n, xs * 2 + oc).astype(BF)
        copy = send(csend.at[h], crecv.at[h], device(flip=True))
        accw[0, :, hc] = dot(dsm[near * 256:, :], qm[h, :, near * HEAD:], 1, 0) * SCALE
        accw[1, :, hc] = dot(pbuf[256:512, :], gm[h, :, near * HEAD:], 1, 0)
        return copy

    def term(h, n, row):
        rows = pl.ds(pl.multiple_of(row * PROWS, PROWS), PROWS)
        return acc[pl.ds(held[n], 1), h, rows, :][0]

    def over_x(h, copy):
        copy.wait_recv()
        for n in range(wide):
            for xs in range(NX):
                total = term(h, n, xs * 2 + c) + crecv[h, xs, n].astype(F32)
                xown[h, xs, n] = total
                xsend[h, xs, n] = total.astype(BF)
        return [
            send(xsend.at[h, lax.rem(x + d, NX)], xrecv.at[h, d - 1], device(dx=d)) for d in (1, 3, 2)
        ]

    def pick(h, target):
        index = jnp.int32(wide)
        for n in range(wide):
            hit = (slot_of[n] == target) & (pg + n < PROMPTS)
            index = jnp.where(hit, n, index)
        return gsum[h, pl.ds(index, 1)][0]

    def over_z(h, copies):
        arrive(copies)
        for n in range(wide):
            total = xown[h, pl.ds(x, 1), n][0]
            for e in range(3):
                total = total + xrecv[h, e, n].astype(F32)
            gsum[h, n] = total
        gsum[h, wide] = jnp.zeros(gsum.shape[2:], F32)
        out = []
        for dz in far:
            zsend[h, dz - 1] = pick(h, lax.rem(z + dz, NZ)).astype(BF)
            out.append(send(zsend.at[h, dz - 1], zrecv.at[h, dz - 1], device(dz=dz)))
        return out

    def yrows(e):
        return pl.ds(pl.multiple_of(lax.rem(y + e, NY) * BLK, 16), BLK)

    def chunk(d):
        both = jnp.concatenate([gqall[d, 0], gqall[d, 1]], axis=1)
        out = dot(wall[...].reshape(NZ * WROWS, QCOLS), both, 1, 0)
        for e in range(2):
            part[d, e] = out[:, e * TOK:(e + 1) * TOK]
            ysend[d, e] = out[:, e * TOK:(e + 1) * TOK].astype(BF)
        up, down = device(dy=1), device(dy=3)
        return [
            send(ysend.at[d, 0, yrows(2)], yrecv.at[d, 0], up),
            send(ysend.at[d, 1, yrows(2)], yrecv.at[d, 1], down),
            send(ysend.at[d, 1, yrows(1)], yrecv.at[d, 2], up),
            send(ysend.at[d, 0, yrows(3)], yrecv.at[d, 3], down),
        ]

    def relay(d, copies):
        copies[0].wait_recv()
        ycomb[d, 0] = (part[d, 0, yrows(1), :] + yrecv[d, 0].astype(F32)).astype(BF)
        copies.append(send(ycomb.at[d, 0], yrecv.at[d, 4], device(dy=1)))
        copies[1].wait_recv()
        ycomb[d, 1] = (part[d, 1, yrows(3), :] + yrecv[d, 1].astype(F32)).astype(BF)
        copies.append(send(ycomb.at[d, 1], yrecv.at[d, 5], device(dy=3)))

    def finish(d, copies):
        arrive(copies[2:])
        own = yrows(0)
        owner_x = lax.rem(x + NX - d, NX)
        out = []
        for e, (a, b) in enumerate(((4, 3), (2, 5))):
            total = part[d, e, own, :] + yrecv[d, a].astype(F32) + yrecv[d, b].astype(F32)
            if d == 0 and e == 0:
                ogi[pl.ds(gidx, 1)] = total.astype(BF)[None]
            else:
                osend[d, e] = total.astype(BF)
                target = (z * 8 + owner_x * 2 + (oc if e else c), y)
                out.append(send(osend.at[d, e], ogi.at[gidx], target))
        return out

    softmax(0)
    gin0 = query_grad(0)
    advance(1, 1)
    c_in0 = key_grad(0)
    softmax(1)
    gin1 = query_grad(1)
    advance(2, 0)
    c_in1 = key_grad(1)
    wsend[...] = accw[:, 0:TOK, :].astype(BF)
    back = send(wsend, wrecv, prv)
    advance(2, 1)
    gx0, gf0 = pass_on(0, gin0)
    store(gq_ref, gq_hbm)
    x_in0 = over_x(0, c_in0)
    advance(3, 0)
    advance(3, 1)
    gx1, gf1 = pass_on(1, gin1)
    x_in1 = over_x(1, c_in1)
    arrive([gin0[0], gin1[0]])
    arrive(ring_in[3, 0] + ring_in[3, 1])
    y0 = chunk(0)
    arrive([gf0[1], gf1[1]])
    y1 = chunk(1)
    arrive([gf0[3], gf1[3]])
    y3 = chunk(3)
    arrive(gx0 + gx1)
    opposite = send(gqall.at[2, 0], gqall.at[2, 1], device(flip=True))
    relay(0, y0)
    arrive([opposite])
    y2 = chunk(2)
    relay(1, y1)
    relay(3, y3)
    z_in0 = over_z(0, x_in0)
    relay(2, y2)
    z_in1 = over_z(1, x_in1)
    o_in = finish(0, y0)
    o_in += finish(1, y1)
    o_in += finish(3, y3)

    back.wait_recv()
    gk_ref[...] = (accw[0, TOK:, :] + wrecv[0].astype(F32)).astype(BF)
    gv_ref[...] = (accw[1, TOK:, :] + wrecv[1].astype(F32)).astype(BF)
    store(gk_ref, gk_hbm)
    store(gv_ref, gv_hbm)
    o_in += finish(2, y2)

    arrive(z_in0 + z_in1)
    for h in range(KVH):
        total = pick(h, z)
        for e in range(NZ - 1):
            total = total + zrecv[h, e].astype(F32)
        gpk_ref[:, h * HEAD:(h + 1) * HEAD] = total[:, 0:HEAD].astype(BF)
        gpv_ref[:, h * HEAD:(h + 1) * HEAD] = total[:, HEAD:].astype(BF)
    store(gpk_ref, gpk_hbm)
    store(gpv_ref, gpv_hbm)

    arrive(o_in)
    blocks = []
    for zz in range(2):
        for j in range(8):
            blocks.append(ogi[j, zz * WROWS:(zz + 1) * WROWS, :])
    git = jnp.concatenate(blocks, axis=0)
    for i in range(QCOLS // HEAD):
        gi_ref[:, i * HEAD:(i + 1) * HEAD] = git[i * HEAD:(i + 1) * HEAD, :].astype(F32).T.astype(BF)
    store(gi_ref, gi_hbm)
    for copy in sent:
        copy.wait_send()
    for copy in stores:
        copy.wait()
    assert count[0] <= nsem


def settle_kernel(count, *refs):
    held = refs[2 * count:3 * count]
    sem = refs[-1]
    inward = [pltpu.make_async_copy(refs[i], held[i], sem.at[0, i]) for i in range(count)]
    for copy in inward:
        copy.start()
    outward = [
        pltpu.make_async_copy(held[i], refs[count + i], sem.at[1, i]) for i in range(count)
    ]
    for i in range(count):
        inward[i].wait()
        outward[i].start()
    for copy in outward:
        copy.wait()


def settle(arrays):
    hb = pl.BlockSpec(memory_space=pl.ANY)
    count = len(arrays)
    return pl.pallas_call(
        functools.partial(settle_kernel, count),
        out_shape=tuple(jax.ShapeDtypeStruct(a.shape, a.dtype) for a in arrays),
        in_specs=[hb] * count,
        out_specs=(hb,) * count,
        scratch_shapes=[pltpu.VMEM(a.shape, a.dtype) for a in arrays]
        + [pltpu.SemaphoreType.DMA((2, count))],
        compiler_params=pltpu.CompilerParams(vmem_limit_bytes=56 * 2**20),
    )(*arrays)


def fused(near, wide, cid, queries, keys, values, output_gradient, pk, pv, weight, lengths, owner):
    nsem = 120
    vm = pl.BlockSpec(memory_space=pltpu.VMEM)
    sm = pl.BlockSpec(memory_space=pltpu.SMEM)
    hb = pl.BlockSpec(memory_space=pl.ANY)
    shape = jax.ShapeDtypeStruct
    results = [(TOK, QCOLS), (TOK, 256), (TOK, 256), (PROWS, 256), (PROWS, 256), (TOK, QCOLS)]
    scratch = [pltpu.VMEM((TOK, QCOLS), BF), pltpu.VMEM((TOK, QCOLS), BF)]
    scratch += [pltpu.VMEM(r, BF) for r in results]
    scratch += [
        pltpu.VMEM((NZ, PROWS, 256), BF),
        pltpu.VMEM((NZ, PROWS, 256), BF),
        pltpu.VMEM((8, wide, PROWS, 256), BF),
        pltpu.VMEM((8, wide, PROWS, 256), BF),
        pltpu.VMEM((2 * TOK, 256), BF),
        pltpu.VMEM((2 * TOK, 256), BF),
        pltpu.VMEM((NZ, WROWS, QCOLS), BF),
        pltpu.VMEM((NX, 2, QCOLS, TOK), BF),
        pltpu.VMEM((KVH, LANES, (near + 1) * HEAD), BF),
        pltpu.VMEM((KVH, LANES, (near + 1) * HEAD), BF),
        pltpu.VMEM((KVH, 512, LANES), F32),
        pltpu.VMEM((KVH, 512, LANES), F32),
        pltpu.VMEM((512, LANES), BF),
        pltpu.VMEM((256, LANES), BF),
        pltpu.VMEM(((near + 1) * 256, LANES), BF),
        pltpu.VMEM((near + 1, KVH, 256, 256), F32),
        pltpu.VMEM((2, 2 * TOK, 256), F32),
        pltpu.VMEM((2, TOK, 256), BF),
        pltpu.VMEM((2, TOK, 256), BF),
        pltpu.VMEM((KVH, NX, wide, PROWS, 256), BF),
        pltpu.VMEM((KVH, NX, wide, PROWS, 256), BF),
        pltpu.VMEM((KVH, NX, wide, PROWS, 256), F32),
        pltpu.VMEM((KVH, NX, wide, PROWS, 256), BF),
        pltpu.VMEM((KVH, NX - 1, wide, PROWS, 256), BF),
        pltpu.VMEM((KVH, wide + 1, PROWS, 256), F32),
        pltpu.VMEM((KVH, NZ - 1, PROWS, 256), BF),
        pltpu.VMEM((KVH, NZ - 1, PROWS, 256), BF),
        pltpu.VMEM((NX, 2, NZ * WROWS, TOK), F32),
        pltpu.VMEM((NX, 2, NZ * WROWS, TOK), BF),
        pltpu.VMEM((NX, 2, BLK, TOK), BF),
        pltpu.VMEM((NX, 6, BLK, TOK), BF),
        pltpu.VMEM((NX, 2, BLK, TOK), BF),
        pltpu.VMEM((8, BLK, TOK), BF),
        pltpu.SemaphoreType.DMA((nsem,)),
        pltpu.SemaphoreType.DMA((nsem,)),
        pltpu.SemaphoreType.DMA((13,)),
    ]
    results = pl.pallas_call(
        functools.partial(kernel, near, wide, nsem),
        out_shape=tuple(shape(r, BF) for r in results),
        in_specs=[hb] * 7 + [vm] + [sm] * 2,
        out_specs=(hb,) * 6,
        scratch_shapes=scratch,
        compiler_params=pltpu.CompilerParams(
            collective_id=cid, has_side_effects=True, vmem_limit_bytes=56 * 2**20
        ),
    )(
        queries, keys, values, output_gradient, pk, pv, weight,
        lengths.reshape(1, RESPONSES), lengths, owner,
    )
    return settle(results)


def few_prompts(lengths):
    tokens = jnp.sum(lengths.reshape(PROMPTS, RESP_PER), axis=1)
    return jnp.min(tokens) >= 4 * TOK


def shards(*args):
    return lax.cond(
        few_prompts(args[7]),
        functools.partial(fused, 2, 3, 0),
        functools.partial(fused, 6, 6, 1),
        *args,
    )


def solution(mesh):
    split = P("dp", "tensor")
    return jax.shard_map(
        shards,
        mesh=mesh,
        in_specs=(split,) * 7 + (P(), P()),
        out_specs=(split,) * 6,
        check_vma=False,
    )
```

time: 79.3 us -> 67.9 us (0.86); the launches traced: 78 us -> 67.7 us
  Pallas kernels: 72 us -> 63.8 us
  local copies, waits for them, and re-layouts: 5.41 us -> 1.44 us
  between operations: 0.67 us -> 1.48 us
    pallas_call x1 -> x2, Pallas kernels: 72 us -> 63.8 us  [the longest x1 61.8 us: fused(): pl.pallas_call(functools.partial(kernel, near, wide, nsem), out_shape=tup...]
    unnamed x16 -> x4, local copies, waits for them, and re-layouts: 5.41 us -> 0.65 us
where the time goes in v2:
time: 67.9 us; the launch traced here: 67.7 us
  Pallas kernels  63.8 us (94%)
  between operations  1.48 us (2%)
  local copies, waits for them, and re-layouts  1.44 us (2%)
  other arithmetic  0.76 us (1%)
    pallas_call x1, Pallas kernels, fused(): pl.pallas_call(functools.partial(kernel, near, wide, nsem), out_shape=tup...  61.8 us
    pallas_call x1, Pallas kernels, settle(): pl.pallas_call(functools.partial(settle_kernel, count), out_shape=tuple((...  2 us

profile of v2, /device:TPU:1, one launch (start us, length us, event | category | flops | bytes accessed | tf_op | source)
XLA Modules:
  0.0 67.7 jit_solution(12855317863486795137)
XLA Ops:
  0.6 0.0 copy-start.2
  0.6 0.6 copy-done.2
  1.3 0.1 reshape.21
  1.4 0.1 reduce_sum.9
  1.5 0.6 reduce_min.9
  2.1 0.0 copy-start.3
  2.8 0.0 copy-done.3
  2.8 64.7 %conditional.1 = ((bf16[128,1280]{1,0:T(8,128)(2,1)}, bf16[128,256]{1,0:T(8,128)(2,1)}, bf16[128,256]{1,0:T(8,128)(2,1)}, bf16[32,256]{1,0:T(8,128)(2,1)}, bf16[...) conditional(s32[]{:T(128)} %convert_element_type.3, (s32[128]{0:T(128)S(1)}, bf16[128,1280]{1,0:T(8,128)(2,1)}, ...), branch_computations={%region_2.0_spmd, %region_3.0_spmd} | conditional | bytes 65572 | solution.py:557
  3.0 0.0 copy-start.1
  3.0 0.7 %copy-done.1 = bf16[32,256]{1,0:T(8,128)(2,1)S(1)} copy-done((bf16[32,256]{1,0:T(8,128)(2,1)S(1)}, bf16[32,256]{1,0:T(8,128)(2,1)}, u32[]{:S(2)}) %copy-start.1) | copy-done | bytes 16408 | tf_op jit(solution)/shard_map/cond
  3.7 61.8 %branch_1_fun.2 = (bf16[128,1280]{1,0:T(8,128)(2,1)}, bf16[128,256]{1,0:T(8,128)(2,1)}, bf16[128,256]{1,0:T(8,128)(2,1)}, bf16[32,256]{1,0:T(8,128)(2,1)}, bf16[...) custom-call(bf16[128,1280]{1,0:T(8,128)(2,1)} %get-tuple-element.51.q_hbm, bf16[128,256]{1,0:T(8,128)(2,1)} %get-tuple-element.52.k_hbm, ...), custom_call_target="tpu_custom_call" | custom-call | tf_op jit(solution)/shard_map/cond/branch_1_fun/pallas_call | solution.py:535
  65.5 2.0 %branch_1_fun.3 = (bf16[128,1280]{1,0:T(8,128)(2,1)}, bf16[128,256]{1,0:T(8,128)(2,1)}, bf16[128,256]{1,0:T(8,128)(2,1)}, bf16[32,256]{1,0:T(8,128)(2,1)}, bf16[...) custom-call(bf16[128,1280]{1,0:T(8,128)(2,1)} %get-tuple-element.60.refs_0_, bf16[128,256]{1,0:T(8,128)(2,1)} %get-tuple-element.61.refs_1_, ...), custom_call_target="tpu_custom_call" | custom-call | tf_op jit(solution)/shard_map/cond/branch_1_fun/pallas_call | solution.py:477
Async XLA Ops:
  0.6 0.7 copy-start.2
  2.1 0.7 copy-start.3
  3.0 0.7 %copy-start.1 = (bf16[32,256]{1,0:T(8,128)(2,1)S(1)}, bf16[32,256]{1,0:T(8,128)(2,1)}, u32[]{:S(2)}) copy-start(bf16[32,256]{1,0:T(8,128)(2,1)} %get-tuple-element.55.pk_hbm) | copy-start | bytes 49156 | tf_op jit(solution)/shard_map/cond

commit v3 on v2

--- a/solution.py
+++ b/solution.py
@@ -396,13 +396,13 @@
     advance(2, 1)
     gx0, gf0 = pass_on(0, gin0)
     store(gq_ref, gq_hbm)
-    x_in0 = over_x(0, c_in0)
     advance(3, 0)
     advance(3, 1)
     gx1, gf1 = pass_on(1, gin1)
-    x_in1 = over_x(1, c_in1)
     arrive([gin0[0], gin1[0]])
     arrive(ring_in[3, 0] + ring_in[3, 1])
+    x_in0 = over_x(0, c_in0)
+    x_in1 = over_x(1, c_in1)
     y0 = chunk(0)
     arrive([gf0[1], gf1[1]])
     y1 = chunk(1)

time: 67.9 us -> 66.4 us (0.978)
  Pallas kernels: 63.8 us -> 62.2 us
    pallas_call x1, Pallas kernels: 61.8 us -> 60.2 us  [fused(): pl.pallas_call(functools.partial(kernel, near, wide, nsem), out_shape=tup...]
where the time goes in v3:
time: 66.4 us; the launch traced here: 66.1 us
  Pallas kernels  62.2 us (94%)
  between operations  1.48 us (2%)
  local copies, waits for them, and re-layouts  1.44 us (2%)
  other arithmetic  0.76 us (1%)
    pallas_call x1, Pallas kernels, fused(): pl.pallas_call(functools.partial(kernel, near, wide, nsem), out_shape=tup...  60.2 us
    pallas_call x1, Pallas kernels, settle(): pl.pallas_call(functools.partial(settle_kernel, count), out_shape=tuple((...  2 us

profile of v3, /device:TPU:1, one launch (start us, length us, event | category | flops | bytes accessed | tf_op | source)
XLA Modules:
  0.0 66.1 jit_solution(3318326054672494887)
XLA Ops:
  0.6 0.0 copy-start.2
  0.6 0.6 copy-done.2
  1.3 0.1 reshape.21
  1.4 0.1 reduce_sum.9
  1.5 0.6 reduce_min.9
  2.1 0.0 copy-start.3
  2.8 0.0 copy-done.3
  2.8 63.2 %conditional.1 = ((bf16[128,1280]{1,0:T(8,128)(2,1)}, bf16[128,256]{1,0:T(8,128)(2,1)}, bf16[128,256]{1,0:T(8,128)(2,1)}, bf16[32,256]{1,0:T(8,128)(2,1)}, bf16[...) conditional(s32[]{:T(128)} %convert_element_type.3, (s32[128]{0:T(128)S(1)}, bf16[128,1280]{1,0:T(8,128)(2,1)}, ...), branch_computations={%region_2.0_spmd, %region_3.0_spmd} | conditional | bytes 65572 | solution.py:557
  3.0 0.0 copy-start.1
  3.0 0.7 %copy-done.1 = bf16[32,256]{1,0:T(8,128)(2,1)S(1)} copy-done((bf16[32,256]{1,0:T(8,128)(2,1)S(1)}, bf16[32,256]{1,0:T(8,128)(2,1)}, u32[]{:S(2)}) %copy-start.1) | copy-done | bytes 16408 | tf_op jit(solution)/shard_map/cond
  3.7 60.2 %branch_1_fun.2 = (bf16[128,1280]{1,0:T(8,128)(2,1)}, bf16[128,256]{1,0:T(8,128)(2,1)}, bf16[128,256]{1,0:T(8,128)(2,1)}, bf16[32,256]{1,0:T(8,128)(2,1)}, bf16[...) custom-call(bf16[128,1280]{1,0:T(8,128)(2,1)} %get-tuple-element.51.q_hbm, bf16[128,256]{1,0:T(8,128)(2,1)} %get-tuple-element.52.k_hbm, ...), custom_call_target="tpu_custom_call" | custom-call | tf_op jit(solution)/shard_map/cond/branch_1_fun/pallas_call | solution.py:535
  64.0 2.0 %branch_1_fun.3 = (bf16[128,1280]{1,0:T(8,128)(2,1)}, bf16[128,256]{1,0:T(8,128)(2,1)}, bf16[128,256]{1,0:T(8,128)(2,1)}, bf16[32,256]{1,0:T(8,128)(2,1)}, bf16[...) custom-call(bf16[128,1280]{1,0:T(8,128)(2,1)} %get-tuple-element.60.refs_0_, bf16[128,256]{1,0:T(8,128)(2,1)} %get-tuple-element.61.refs_1_, ...), custom_call_target="tpu_custom_call" | custom-call | tf_op jit(solution)/shard_map/cond/branch_1_fun/pallas_call | solution.py:477
Async XLA Ops:
  0.6 0.7 copy-start.2
  2.1 0.7 %copy-start.3 = (s32[8]{0:T(128)S(1)}, s32[8]{0:T(128)}, u32[]{:S(2)}) copy-start(s32[8]{0:T(128)} %param.19) | copy-start | bytes 100
  3.0 0.7 %copy-start.1 = (bf16[32,256]{1,0:T(8,128)(2,1)S(1)}, bf16[32,256]{1,0:T(8,128)(2,1)}, u32[]{:S(2)}) copy-start(bf16[32,256]{1,0:T(8,128)(2,1)} %get-tuple-element.55.pk_hbm) | copy-start | bytes 49156 | tf_op jit(solution)/shard_map/cond

commit v4 on v3

--- a/solution.py
+++ b/solution.py
@@ -481,7 +481,7 @@
         out_specs=(hb,) * count,
         scratch_shapes=[pltpu.VMEM(a.shape, a.dtype) for a in arrays]
         + [pltpu.SemaphoreType.DMA((2, count))],
-        compiler_params=pltpu.CompilerParams(vmem_limit_bytes=56 * 2**20),
+        compiler_params=pltpu.CompilerParams(vmem_limit_bytes=64 * 2**20),
     )(*arrays)
 
 
@@ -539,7 +539,7 @@
         out_specs=(hb,) * 6,
         scratch_shapes=scratch,
         compiler_params=pltpu.CompilerParams(
-            collective_id=cid, has_side_effects=True, vmem_limit_bytes=56 * 2**20
+            collective_id=cid, has_side_effects=True, vmem_limit_bytes=64 * 2**20
         ),
     )(
         queries, keys, values, output_gradient, pk, pv, weight,

time: 66.4 us -> 66 us (level)
  local copies, waits for them, and re-layouts: 1.44 us -> 0.73 us
    cond x2 -> x0, local copies, waits for them, and re-layouts: 0.71 us -> none
where the time goes in v4:
time: 66 us; the launch traced here: 65.8 us
  Pallas kernels  62.7 us (95%)
  between operations  1.45 us (2%)
  other arithmetic  0.76 us (1%)
  local copies, waits for them, and re-layouts  0.73 us (1%)
    pallas_call x1, Pallas kernels, fused(): pl.pallas_call(functools.partial(kernel, near, wide, nsem), out_shape=tup...  60.7 us
    pallas_call x1, Pallas kernels, settle(): pl.pallas_call(functools.partial(settle_kernel, count), out_shape=tuple((...  2 us

profile of v4, /device:TPU:1, one launch (start us, length us, event | category | flops | bytes accessed | tf_op | source)
XLA Modules:
  0.0 65.8 jit_solution(875095460790273070)
XLA Ops:
  0.6 0.7 %reshape.21 = s32[8,16]{1,0:T(8,128)S(1)} reshape(s32[128]{0:T(128)} %param.18) | data formatting | bytes 1024 | tf_op jit(solution)/shard_map/reshape | solution.py:552
  1.4 0.1 reduce_sum.9
  1.5 0.6 reduce_min.9
  2.8 62.9 %conditional.1 = ((bf16[128,1280]{1,0:T(8,128)(2,1)}, bf16[128,256]{1,0:T(8,128)(2,1)}, bf16[128,256]{1,0:T(8,128)(2,1)}, bf16[32,256]{1,0:T(8,128)(2,1)}, bf16[...) conditional(s32[]{:T(128)} %convert_element_type.3, (s32[128]{0:T(128)}, bf16[128,1280]{1,0:T(8,128)(2,1)}, ...), branch_computations={%region_2.0_spmd, %region_3.0_spmd} | conditional | bytes 8 | solution.py:557
  3.0 60.7 %branch_1_fun.2 = (bf16[128,1280]{1,0:T(8,128)(2,1)}, bf16[128,256]{1,0:T(8,128)(2,1)}, bf16[128,256]{1,0:T(8,128)(2,1)}, bf16[32,256]{1,0:T(8,128)(2,1)}, bf16[...) custom-call(bf16[128,1280]{1,0:T(8,128)(2,1)} %get-tuple-element.51.q_hbm, bf16[128,256]{1,0:T(8,128)(2,1)} %get-tuple-element.52.k_hbm, ...), custom_call_target="tpu_custom_call" | custom-call | tf_op jit(solution)/shard_map/cond/branch_1_fun/pallas_call | solution.py:535
  63.6 2.0 %branch_1_fun.3 = (bf16[128,1280]{1,0:T(8,128)(2,1)}, bf16[128,256]{1,0:T(8,128)(2,1)}, bf16[128,256]{1,0:T(8,128)(2,1)}, bf16[32,256]{1,0:T(8,128)(2,1)}, bf16[...) custom-call(bf16[128,1280]{1,0:T(8,128)(2,1)} %get-tuple-element.60.refs_0_, bf16[128,256]{1,0:T(8,128)(2,1)} %get-tuple-element.61.refs_1_, ...), custom_call_target="tpu_custom_call" | custom-call | tf_op jit(solution)/shard_map/cond/branch_1_fun/pallas_call | solution.py:477
